TPU v7x, 32 devices: a whole 2x2x4 slice. The times are simulated.
32 devices in a mesh: dp: 8 (over y, x, core), expert: 4 (over z).
Axes of the slice: x: 2, y: 2, z: 4, core: 2. Of those that a mesh axis runs over, the one named last changes fastest.
Arguments:
- tokens: bfloat16 [4096, 4096], P(('dp', 'expert')), may hold values from -6 to 6
- expert_ids: int32 [4096, 8], P(('dp', 'expert')), may hold values from 0 to 31, all different within a row; in each aligned block of 128 rows (0 to 127, 128 to 255, ...) at most 48 rows name the same one
- route_weight: float32 [4096, 8], P(('dp', 'expert')), may hold values from 0.05 to 1
- w_gate: bfloat16 [32, 4096, 768], P(('dp', 'expert')), may hold values from -0.09375 to 0.09375
- w_up: bfloat16 [32, 4096, 768], P(('dp', 'expert')), may hold values from -0.09375 to 0.09375
- w_down: bfloat16 [32, 768, 4096], P(('dp', 'expert')), may hold values from -0.21875 to 0.21875
Outputs:
- moe_out: bfloat16 [4096, 4096], P(('dp', 'expert'))
Inputs may be any that keep to these rules, and one draw needn't show every extreme that they name: `expert_ids`: each row names 8 different experts; in the rows of one device no expert is named more than 48 times.
All inputs are finite; a program needn't handle non-finite values.
Results may differ from a plain program's by a relative error of at most 0.008.
Values may be sent and summed in bfloat16 or wider, within the bound.
A program may use at most 128 MiB of HBM per device.

v0:
```python
import jax
import jax.numpy as jnp
from jax import lax
from jax.sharding import PartitionSpec as P


def body(tokens, expert_ids, route_weight, w_gate, w_up, w_down):
    tok_dev, width = tokens.shape
    top_count = expert_ids.shape[1]
    dp_count = lax.axis_size("dp")
    ex_count = lax.axis_size("expert")
    experts = dp_count * ex_count
    capacity = tok_dev * top_count * 3 // (2 * experts)
    flat_ids = expert_ids.reshape(-1)
    one_hot = (flat_ids[:, None] == jnp.arange(experts, dtype=jnp.int32)[None, :]).astype(jnp.int32)
    earlier = jnp.cumsum(one_hot, axis=0) - one_hot
    slot_index = jnp.sum(earlier * one_hot, axis=1)
    position = flat_ids * capacity + slot_index
    source_row = jnp.arange(tok_dev * top_count, dtype=jnp.int32) // top_count
    slot_table = jnp.zeros((experts * capacity,), jnp.int32).at[position].set(source_row + 1)
    filled = slot_table > 0
    gathered = tokens[jnp.maximum(slot_table - 1, 0)]
    outgoing = jnp.where(filled[:, None], gathered, jnp.zeros_like(gathered))
    per_dest = outgoing.reshape(experts, capacity, width)
    arrived = lax.all_to_all(per_dest, ("dp", "expert"), split_axis=0, concat_axis=0, tiled=True)
    flat_rows = arrived.reshape(-1, width)
    gate_act = jnp.dot(flat_rows, w_gate[0], preferred_element_type=jnp.float32)
    up_act = jnp.dot(flat_rows, w_up[0], preferred_element_type=jnp.float32)
    hidden = (jax.nn.silu(gate_act) * up_act).astype(jnp.bfloat16)
    projected = jnp.dot(hidden, w_down[0], preferred_element_type=jnp.float32).astype(jnp.bfloat16)
    results = projected.reshape(arrived.shape)
    returned_rows = lax.all_to_all(
        results, ("dp", "expert"), split_axis=0, concat_axis=0, tiled=True
    )
    picked = returned_rows.reshape(experts * capacity, width)[position]
    picked = picked.reshape(tok_dev, top_count, width)
    weighted = jnp.einsum("tkd,tk->td", picked, route_weight, preferred_element_type=jnp.float32)
    return weighted.astype(jnp.bfloat16)


def solution(mesh):
    placed = (
        P(("dp", "expert"), None),
        P(("dp", "expert"), None),
        P(("dp", "expert"), None),
        P(("dp", "expert"), None, None),
        P(("dp", "expert"), None, None),
        P(("dp", "expert"), None, None),
    )
    return jax.shard_map(
        body, mesh=mesh, in_specs=placed, out_specs=P(("dp", "expert"), None), check_vma=False
    )
```

profile of v0, /device:TPU:0, one launch (start us, length us, event | category | flops | bytes accessed | tf_op | source)
XLA Modules:
  0.0 653.3 jit_solution(1082615811590234777)
XLA Ops:
  0.0 0.0 copy-start
  0.0 0.9 copy.8
  0.9 0.1 eq.29
  1.0 0.1 eq.25
  1.1 0.7 broadcast_multiply_fusion
  1.8 9.0 %reduce-window.6 = s32[32,8,128]{2,1,0:T(8,128)S(1)} reduce-window(s32[32,8,128]{2,1,0:T(8,128)S(1)} %fusion.12, s32[]{:T(128)} %constant.30.clone.1), window={size=1x1x128 pad=0_0x0_0x127_0}, to_apply=%region_0.0 | reduce-window | flops 4161536 | bytes 262148 | tf_op jit(solution)/shard_map/reduce-window
  10.8 0.1 slice.12
  10.9 0.1 copy.10
  11.1 0.1 copy.11
  11.1 0.1 broadcast_add_fusion
  11.2 0.1 copy.7
  11.3 0.1 mul.28
  11.5 4.3 scatter_custom_fusion
  15.9 0.1 broadcast_in_dim.20
  16.0 0.0 copy-done
  16.0 9.5 %gather_fusion = bf16[1536,4096]{1,0:T(8,128)(2,1)} fusion(bf16[128,4096]{1,0:T(8,128)(2,1)S(1)} %copy-done, s32[2048]{0:T(1024)S(1)} %pad_clamp_fusion), kind=kCustom, calls=%fused_computation | custom fusion | bytes 25171968 | tf_op jit(solution)/shard_map/gather | solution.py:22
  25.5 6.4 broadcast_select_fusion
  31.9 0.0 copy-start.3
  31.9 279.3 %all_to_all.10 = bf16[32,48,4096]{2,1,0:T(8,128)(2,1)S(1)} all-to-all(bf16[32,48,4096]{2,1,0:T(8,128)(2,1)S(1)} %broadcast_select_fusion), channel_id=1, replica_groups=mesh['dp'=8,'expert'=4] {'dp','expert'}, dimensions={0} | all-to-all | bytes 25165824 | tf_op jit(solution)/shard_map/all_to_all | solution.py:25
  311.2 0.0 copy-done.3
  311.2 11.4 %fusion.3 = f32[1536,768]{1,0:T(8,128)} fusion(bf16[1536,4096]{1,0:T(8,128)(2,1)S(1)} %bitcast.48, bf16[1,4096,768]{2,1,0:T(8,128)(2,1)S(1)} %copy-done.3), kind=kOutput, calls=%fused_computation.8 | convolution fusion | flops 9663676416 | bytes 23592960 | tf_op jit(solution)/shard_map/dot_general | solution.py:28
  322.7 13.5 %multiply_convert_fusion = bf16[1536,768]{1,0:T(8,128)(2,1)S(1)} fusion(f32[1536,768]{1,0:T(8,128)} %fusion.3, bf16[1536,4096]{1,0:T(8,128)(2,1)S(1)} %bitcast.49, bf16[1,4096,768]{2,1,0:T(8,128)(2,1)} %param.9), kind=kOutput, calls=%fused_computation.12 | convolution fusion | flops 9670754304 | bytes 25952256 | tf_op jit(solution)/shard_map/dot_general | solution.py:27
  336.2 0.0 slice-done
  336.2 0.0 slice-done.1
  336.2 12.4 %convolution_convert_fusion = bf16[1536,4096]{1,0:T(8,128)(2,1)} fusion(bf16[1536,768]{1,0:T(8,128)(2,1)S(1)} %multiply_convert_fusion, bf16[1,768,4096]{2,1,0:T(8,128)(2,1)S(1)} %bitcast.57), kind=kOutput, calls=%fused_computation.3 | convolution fusion | flops 9669967872 | bytes 21233664 | tf_op jit(solution)/shard_map/dot_general | solution.py:30
  348.6 4.8 all-to-all-start.1
  353.4 0.0 copy-done.2
  353.4 0.1 copy.12
  353.5 270.5 %all-to-all-done.1 = bf16[32,48,4096]{2,1,0:T(8,128)(2,1)} async-done(((bf16[32,48,4096]{2,1,0:T(8,128)(2,1)}), bf16[32,48,4096]{2,1,0:T(8,128)(2,1)}, u32[]{:S(2)}, u32[]{:S(2)}) %all-to-all-start.1) | async-done | bytes 12582944 | tf_op jit(solution)/shard_map/all_to_all | solution.py:32
  624.1 21.4 %gather_fusion.1 = bf16[1024,4096]{1,0:T(8,128)(2,1)} fusion(bf16[1536,4096]{1,0:T(8,128)(2,1)} %bitcast.10, s32[1024]{0:T(1024)S(1)} %broadcast_clamp_fusion), kind=kCustom, calls=%fused_computation.1 | custom fusion | bytes 16781312 | tf_op jit(solution)/shard_map/gather | solution.py:35
  645.4 5.7 fusion
  651.1 2.1 copy.17
  (16 shorter events, 0.1 us)
Async XLA Ops:
  0.0 16.0 %copy-start = (bf16[128,4096]{1,0:T(8,128)(2,1)S(1)}, bf16[128,4096]{1,0:T(8,128)(2,1)}, u32[]{:S(2)}) copy-start(bf16[128,4096]{1,0:T(8,128)(2,1)} %param.6) | copy-start | bytes 3145732
  31.9 279.4 %copy-start.3 = (bf16[1,4096,768]{2,1,0:T(8,128)(2,1)S(1)}, bf16[1,4096,768]{2,1,0:T(8,128)(2,1)}, u32[]{:S(2)}) copy-start(bf16[1,4096,768]{2,1,0:T(8,128)(2,1)} %param.10) | copy-start | bytes 18874372
  311.2 24.9 %slice-start = ((s8[6291456]{0:T(1024)(128)(4,1)}), s8[2097152]{0:T(1024)(128)(4,1)S(1)}, s32[]{:S(2)}) async-start(s8[6291456]{0:T(1024)(128)(4,1)} %bitcast.56), calls=%async_computation.2 | async-start | bytes 4194304
  322.7 13.5 %slice-start.1 = ((s8[6291456]{0:T(1024)(128)(4,1)}), s8[4194304]{0:T(1024)(128)(4,1)S(1)}, s32[]{:S(2)}) async-start(s8[6291456]{0:T(1024)(128)(4,1)} %bitcast.56), calls=%async_computation.3 | async-start | bytes 8388608
  348.6 4.8 copy-start.2
  348.6 275.5 %all-to-all-start.1 = ((bf16[32,48,4096]{2,1,0:T(8,128)(2,1)}), bf16[32,48,4096]{2,1,0:T(8,128)(2,1)}, u32[]{:S(2)}, u32[]{:S(2)}) async-start(bf16[32,48,4096]{2,1,0:T(8,128)(2,1)} %bitcast.47), calls=%async_computation.1 | async-start | bytes 25165824 | tf_op jit(solution)/shard_map/all_to_all | solution.py:32
  624.1 29.2 %copy-start.1 = (bf16[128,4096]{1,0:T(8,128)(2,1)S(1)}, bf16[128,4096]{1,0:T(8,128)(2,1)}, u32[]{:S(2)}) copy-start(bf16[128,4096]{1,0:T(8,128)(2,1)} %param.6) | copy-start | bytes 3145732
where the time goes:
time: 660 us; the launch traced here: 653 us
  blocking collectives  279 us (42%)
  waiting for transfers between devices  271 us (41%)
  matrix products  43 us (7%)
  local copies, waits for them, and re-layouts  39.1 us (6%)
  other arithmetic  16.3 us (2%)
    all_to_all x1, blocking collectives, body(): lax.all_to_all(per_dest, ('dp', 'expert'), split_axis=0, concat_axis=0, t...  279 us
    all_to_all x1, waiting for transfers between devices, body(): lax.all_to_all(results, ('dp', 'expert'), split_axis=0, concat_axis=0, ti...  271 us
    gather x1, local copies, waits for them, and re-layouts, body(): picked = returned_rows.reshape(experts * capacity, width)[position]  21.4 us
    dot_general x1, matrix products, body(): gate_act = jnp.dot(flat_rows, w_gate[0], preferred_element_type=jnp.float32)  13.5 us
  transfers between devices with their start and end apart: 1, of which 1 were waited for; matrix products, arithmetic and copies ran while one was open for 0% of the time, Pallas kernels for 0%

commit v1 on v0

v1 whole, which is shorter than its diff:
```python
import functools

import jax
import jax.numpy as jnp
from jax import lax
from jax.experimental import pallas as pl
from jax.experimental.pallas import tpu as pltpu
from jax.sharding import PartitionSpec as P

MESH = pl.DeviceIdType.MESH


def tile_of(extent, most):
    return most if extent % most == 0 else extent


def kernel(
    dp_count,
    ex_count,
    cap,
    tok_ref,
    wt_ref,
    wg_hbm,
    wu_hbm,
    wd_hbm,
    out_ref,
    zt,
    ret,
    wg,
    wu,
    wd,
    zw,
    tok,
    send,
    recv,
    hid,
    zret,
    weight_sem,
    local_sem,
    zt_send,
    zt_recv,
    zw_send,
    zw_recv,
    send_sem,
    recv_sem,
    back_send,
    back_recv,
    zret_send,
    zret_recv,
):
    p = lax.axis_index("dp")
    z = lax.axis_index("expert")
    width = tok_ref.shape[1]
    ff = wg.shape[1]
    tok_dev = tok_ref.shape[0]
    mine = pl.ds(pl.multiple_of(p * cap, cap), cap)
    others = pl.ds(0, (dp_count - 1) * cap)
    ff_tile = tile_of(ff, 256)
    col_tile = tile_of(width, 512)

    loads = [
        pltpu.make_async_copy(src, dst, weight_sem.at[i])
        for i, (src, dst) in enumerate(((wg_hbm, wg), (wu_hbm, wu), (wd_hbm, wd)))
    ]
    own = pltpu.make_async_copy(tok_ref, tok, local_sem.at[0])
    own.start()
    own_wt = pltpu.make_async_copy(wt_ref.at[z], zw.at[0], local_sem.at[1])
    own_wt.start()
    for load in loads:
        load.start()

    barrier = pltpu.get_barrier_semaphore()
    for d in range(1, dp_count):
        pl.semaphore_signal(barrier, inc=1, device_id=((p + d) % dp_count, z), device_id_type=MESH)
    for d in range(1, ex_count):
        pl.semaphore_signal(barrier, inc=1, device_id=(p, (z + d) % ex_count), device_id_type=MESH)
    pl.semaphore_wait(barrier, dp_count + ex_count - 2)

    def token_copy(d):
        return pltpu.make_async_remote_copy(
            src_ref=tok_ref,
            dst_ref=zt.at[d],
            send_sem=zt_send.at[d],
            recv_sem=zt_recv.at[d],
            device_id=(p, (z + d) % ex_count),
            device_id_type=MESH,
        )

    def table_copy(d):
        target = (z + d) % ex_count
        return pltpu.make_async_remote_copy(
            src_ref=wt_ref.at[target],
            dst_ref=zw.at[d],
            send_sem=zw_send.at[d],
            recv_sem=zw_recv.at[d],
            device_id=(p, target),
            device_id_type=MESH,
        )

    def partial_copy(t):
        return pltpu.make_async_remote_copy(
            src_ref=recv.at[t, pl.ds(0, tok_dev)],
            dst_ref=zret.at[t],
            send_sem=zret_send.at[t],
            recv_sem=zret_recv.at[t],
            device_id=(p, (z + ex_count - t) % ex_count),
            device_id_type=MESH,
        )

    def wait_for(ref, sem):
        pltpu.make_async_copy(ref, ref, sem).wait()

    for d in range(1, ex_count):
        table_copy(d).start()
        token_copy(d).start()

    def dispatch(t):
        slot = lax.rem(t, 2)
        table = (zw[t] > 0.0).astype(jnp.bfloat16)

        @pl.loop(0, width // col_tile)
        def _(i):
            cols = pl.ds(pl.multiple_of(i * col_tile, col_tile), col_tile)
            rows = jnp.dot(table, tok[:, cols], preferred_element_type=jnp.float32)
            send[slot, :, cols] = rows.astype(jnp.bfloat16)

        for d in range(1, dp_count):
            peer = (p + d) % dp_count
            pltpu.make_async_remote_copy(
                src_ref=send.at[slot, pl.ds(pl.multiple_of(peer * cap, cap), cap)],
                dst_ref=recv.at[t, mine],
                send_sem=send_sem.at[slot],
                recv_sem=recv_sem.at[t],
                device_id=(peer, z),
                device_id_type=MESH,
            ).start()
        keep = pltpu.make_async_copy(send.at[slot, mine], recv.at[t, mine], local_sem.at[0])
        keep.start()
        keep.wait()

    def arrived(t):
        token_copy(t).wait_recv()
        table_copy(t).wait_recv()
        load = pltpu.make_async_copy(zt.at[t], tok, local_sem.at[0])
        load.start()
        load.wait()

    def expert(t):
        wait_for(recv.at[t, others], recv_sem.at[t])

        @pl.loop(0, ff // ff_tile)
        def _(i):
            cols = pl.ds(pl.multiple_of(i * ff_tile, ff_tile), ff_tile)
            gate = jnp.dot(recv[t], wg[:, cols], preferred_element_type=jnp.float32)
            up = jnp.dot(recv[t], wu[:, cols], preferred_element_type=jnp.float32)
            hid[:, cols] = (gate / (1.0 + jnp.exp(-gate)) * up).astype(jnp.bfloat16)

        @pl.loop(0, width // col_tile)
        def _(i):
            cols = pl.ds(pl.multiple_of(i * col_tile, col_tile), col_tile)
            rows = jnp.dot(hid[...], wd[:, cols], preferred_element_type=jnp.float32)
            recv[t, :, cols] = rows.astype(jnp.bfloat16)

        for d in range(1, dp_count):
            peer = (p + d) % dp_count
            pltpu.make_async_remote_copy(
                src_ref=recv.at[t, pl.ds(pl.multiple_of(peer * cap, cap), cap)],
                dst_ref=ret.at[t, mine],
                send_sem=back_send.at[t],
                recv_sem=back_recv.at[t],
                device_id=(peer, z),
                device_id_type=MESH,
            ).start()
        keep = pltpu.make_async_copy(recv.at[t, mine], ret.at[t, mine], local_sem.at[0])
        keep.start()
        keep.wait()

    def combined(t, store):
        wait_for(ret.at[t, others], back_recv.at[t])
        load = pltpu.make_async_copy(ret.at[t], send.at[0], local_sem.at[0])
        load.start()
        wait_for(recv.at[t, others], back_send.at[t])
        load.wait()
        weight = zw[t].T
        high = weight.astype(jnp.bfloat16)
        low = (weight - high.astype(jnp.float32)).astype(jnp.bfloat16)

        @pl.loop(0, width // col_tile)
        def _(i):
            cols = pl.ds(pl.multiple_of(i * col_tile, col_tile), col_tile)
            rows = send[0, :, cols]
            total = jnp.dot(high, rows, preferred_element_type=jnp.float32)
            total = total + jnp.dot(low, rows, preferred_element_type=jnp.float32)
            store(cols, total)

    own.wait()
    own_wt.wait()
    dispatch(0)
    arrived(1)
    dispatch(1)
    for load in loads:
        load.wait()

    def middle(t, carry):
        arrived(t)
        wait_for(send.at[lax.rem(t, 2), others], send_sem.at[lax.rem(t, 2)])
        dispatch(t)
        expert(t - 1)
        return carry

    lax.fori_loop(2, ex_count, middle, 0)

    def last(t, carry):
        expert(lax.rem(t, ex_count))
        return carry

    lax.fori_loop(ex_count - 1, ex_count + 1, last, 0)
    for slot in range(2):
        wait_for(send.at[slot, others], send_sem.at[slot])

    def home(t, carry):
        def store(cols, total):
            recv[t, pl.ds(0, tok_dev), cols] = total.astype(jnp.bfloat16)

        combined(t, store)
        partial_copy(t).start()
        return carry

    lax.fori_loop(1, ex_count, home, 0)

    for d in range(1, ex_count):
        partial_copy(d).wait_recv()

    def finish(cols, total):
        for d in range(1, ex_count):
            total = total + zret[d, :, cols].astype(jnp.float32)
        out_ref[:, cols] = total.astype(jnp.bfloat16)

    combined(0, finish)

    for d in range(1, ex_count):
        token_copy(d).wait_send()
        table_copy(d).wait_send()
        partial_copy(d).wait_send()


def body(tokens, expert_ids, route_weight, w_gate, w_up, w_down):
    tok_dev, width = tokens.shape
    top_count = expert_ids.shape[1]
    ff = w_gate.shape[2]
    dp_count = lax.axis_size("dp")
    ex_count = lax.axis_size("expert")
    experts = dp_count * ex_count
    needed = tok_dev * top_count * 3 // (2 * experts)
    cap = -(-needed // 16) * 16
    rows = dp_count * cap

    named = expert_ids.T[None, :, :] == jnp.arange(experts, dtype=jnp.int32)[:, None, None]
    chosen = jnp.any(named, axis=1)
    weight = jnp.sum(jnp.where(named, route_weight.T[None, :, :], 0.0), axis=1)
    index = jnp.arange(tok_dev, dtype=jnp.int32)
    before = (index[:, None] < index[None, :]).astype(jnp.bfloat16)
    slot = jnp.dot(chosen.astype(jnp.bfloat16), before, preferred_element_type=jnp.float32)
    slot = jnp.where(chosen, slot.astype(jnp.int32), -1)

    def by_plane(v):
        return v.reshape(dp_count, ex_count, 1, tok_dev).transpose(1, 0, 2, 3)

    at_slot = by_plane(slot) == jnp.arange(cap, dtype=jnp.int32)[None, None, :, None]
    table = jnp.where(at_slot, by_plane(weight), 0.0).reshape(ex_count, rows, tok_dev)

    any_space = pl.BlockSpec(memory_space=pl.ANY)
    vmem = pl.BlockSpec(memory_space=pltpu.VMEM)
    dma = pltpu.SemaphoreType.DMA
    out, _, _ = pl.pallas_call(
        functools.partial(kernel, dp_count, ex_count, cap),
        out_shape=(
            jax.ShapeDtypeStruct((tok_dev, width), jnp.bfloat16),
            jax.ShapeDtypeStruct((ex_count, tok_dev, width), jnp.bfloat16),
            jax.ShapeDtypeStruct((ex_count, rows, width), jnp.bfloat16),
        ),
        in_specs=[any_space, any_space, any_space, any_space, any_space],
        out_specs=(vmem, any_space, any_space),
        scratch_shapes=[
            pltpu.VMEM((width, ff), jnp.bfloat16),
            pltpu.VMEM((width, ff), jnp.bfloat16),
            pltpu.VMEM((ff, width), jnp.bfloat16),
            pltpu.VMEM((ex_count, rows, tok_dev), jnp.float32),
            pltpu.VMEM((tok_dev, width), jnp.bfloat16),
            pltpu.VMEM((2, rows, width), jnp.bfloat16),
            pltpu.VMEM((ex_count, rows, width), jnp.bfloat16),
            pltpu.VMEM((rows, ff), jnp.bfloat16),
            pltpu.VMEM((ex_count, tok_dev, width), jnp.bfloat16),
            dma((3,)),
            dma((2,)),
            dma((ex_count,)),
            dma((ex_count,)),
            dma((ex_count,)),
            dma((ex_count,)),
            dma((2,)),
            dma((ex_count,)),
            dma((ex_count,)),
            dma((ex_count,)),
            dma((ex_count,)),
            dma((ex_count,)),
        ],
        compiler_params=pltpu.CompilerParams(
            collective_id=0, has_side_effects=True, vmem_limit_bytes=60 * 1024 * 1024
        ),
        cost_estimate=pl.CostEstimate(
            flops=6 * ex_count * rows * width * ff,
            bytes_accessed=6 * width * ff + 6 * ex_count * rows * width,
            transcendentals=ex_count * rows * ff,
        ),
    )(tokens, table, w_gate[0], w_up[0], w_down[0])
    return out


def solution(mesh):
    placed = (
        P(("dp", "expert"), None),
        P(("dp", "expert"), None),
        P(("dp", "expert"), None),
        P(("dp", "expert"), None, None),
        P(("dp", "expert"), None, None),
        P(("dp", "expert"), None, None),
    )
    return jax.shard_map(
        body, mesh=mesh, in_specs=placed, out_specs=P(("dp", "expert"), None), check_vma=False
    )
```

time: 660 us -> 331 us (0.50)
  Pallas kernels: 0 us -> 322 us
  blocking collectives: 279 us -> 0 us
  waiting for transfers between devices: 271 us -> 0 us
  matrix products: 43 us -> 0.14 us
  local copies, waits for them, and re-layouts: 39.1 us -> 2.38 us
  other arithmetic: 16.3 us -> 2.49 us
    pallas_call x0 -> x1, Pallas kernels: none -> 322 us  [body(): pl.pallas_call(functools.partial(kernel, dp_count, ex_count, cap), out_sh...]
    all_to_all x1 -> x0, blocking collectives: 279 us -> none  [body(): lax.all_to_all(per_dest, ('dp', 'expert'), split_axis=0, concat_axis=0, t...]
    all_to_all x1 -> x0, waiting for transfers between devices: 271 us -> none  [body(): lax.all_to_all(results, ('dp', 'expert'), split_axis=0, concat_axis=0, ti...]
    dot_general x4 -> x1, matrix products: 43 us -> 0.14 us  [body(): jnp.dot(chosen.astype(jnp.bfloat16), before, preferred_element_type=jnp.f...]
    gather x2 -> x0, local copies, waits for them, and re-layouts: 30.9 us -> none  [the longest x1 21.4 us: body(): picked = returned_rows.reshape(experts * capacity, width)[position]]
    another operation x3 -> x0, other arithmetic: 9.15 us -> none
  transfers between devices with their start and end apart: 1 -> 0, of which waited for: 1 -> 0; matrix products, arithmetic and copies ran while one was open for 0% -> 0% of each run, Pallas kernels for 0% -> 0%
where the time goes in v1:
time: 331 us; the launch traced here: 327 us
  Pallas kernels  322 us (97%)
    pallas_call x1, Pallas kernels, body(): pl.pallas_call(functools.partial(kernel, dp_count, ex_count, cap), out_sh...  322 us

profile of v1, /device:TPU:0, one launch (start us, length us, event | category | flops | bytes accessed | tf_op | source)
XLA Modules:
  0.0 327.1 jit_solution(10525489357073221436)
XLA Ops:
  0.0 0.7 fusion.1
  0.7 0.1 eq.42
  0.8 0.1 fusion
  1.0 0.8 select_reduce_fusion
  1.7 1.0 bitcast_select_fusion.wt_ref
  2.7 322.1 %shard_map.64 = (bf16[128,4096]{1,0:T(8,128)(2,1)}, bf16[4,128,4096]{2,1,0:T(8,128)(2,1)}, bf16[4,384,4096]{2,1,0:T(8,128)(2,1)}) custom-call(bf16[128,4096]{1,0:T(8,128)(2,1)} %tok_ref.1, f32[4,384,128]{2,1,0:T(8,128)} %bitcast_select_fusion.wt_ref, bf16[4096,768]{1,0:T(8,128)(2,1)} %bitcast.27, bf16[4096,768]{1,0:T(8,128)(2,1)} %bitcast.28, ...), custom_call_target="tpu_custom_call" | custom-call | flops 28991029248 | bytes 56623104 | tf_op jit(solution)/shard_map/pallas_call | solution.py:275
  324.8 2.3 copy.13
  (3 shorter events, 0.0 us)

commit v2 on v1

v2 whole, which is shorter than its diff:
```python
import functools

import jax
import jax.numpy as jnp
from jax import lax
from jax.experimental import pallas as pl
from jax.experimental.pallas import tpu as pltpu
from jax.sharding import PartitionSpec as P

MESH = pl.DeviceIdType.MESH


def tile_of(extent, most):
    return most if extent % most == 0 else extent


def kernel(
    dp_count,
    ex_count,
    cap,
    tok_ref,
    meta_ref,
    wg_hbm,
    wu_hbm,
    wd_hbm,
    out_ref,
    zt,
    xt,
    ret,
    wg,
    wu,
    wd,
    zm,
    xm,
    pick,
    share,
    tok,
    send,
    recv,
    hid,
    pret,
    zret,
    weight_sem,
    local_sem,
    zt_send,
    zt_recv,
    zm_send,
    zm_recv,
    xt_send,
    xt_recv,
    xm_send,
    xm_recv,
    send_sem,
    recv_sem,
    back_send,
    back_recv,
    pret_send,
    pret_recv,
    zret_send,
    zret_recv,
):
    p = lax.axis_index("dp")
    z = lax.axis_index("expert")
    group = dp_count // 4
    c = p % group
    b = (p // group) % 2
    a = p // (2 * group)
    odd = c % 2

    def device(row, column, member):
        return (row * 2 + column) * group + member

    first = device(a + odd * (1 - 2 * a), b + (1 - odd) * (1 - 2 * b), c)
    row2, column2 = a + (1 - odd) * (1 - 2 * a), b + odd * (1 - 2 * b)
    width = tok_ref.shape[1]
    ff = wg.shape[1]
    tok_dev = tok_ref.shape[0]
    part = 2 * cap
    others = pl.ds(0, (2 * group - 1) * part)
    ff_tile = tile_of(ff, 256)
    col_tile = tile_of(width, 512)

    def section(i):
        return pl.ds(pl.multiple_of(i * part, part), part)

    loads = [
        pltpu.make_async_copy(src, dst, weight_sem.at[i])
        for i, (src, dst) in enumerate(((wg_hbm, wg), (wu_hbm, wu), (wd_hbm, wd)))
    ]
    own = pltpu.make_async_copy(tok_ref, tok.at[pl.ds(0, tok_dev)], local_sem.at[0])
    own.start()
    own_meta = pltpu.make_async_copy(meta_ref.at[z], zm.at[0], local_sem.at[1])
    own_meta.start()
    for load in loads:
        load.start()

    barrier = pltpu.get_barrier_semaphore()
    for d in range(1, dp_count):
        pl.semaphore_signal(barrier, inc=1, device_id=((p + d) % dp_count, z), device_id_type=MESH)
    for d in range(1, ex_count):
        pl.semaphore_signal(barrier, inc=1, device_id=(p, (z + d) % ex_count), device_id_type=MESH)
    pick[...] = jnp.zeros_like(pick)
    share[...] = jnp.zeros_like(share)
    pl.semaphore_wait(barrier, dp_count + ex_count - 2)

    def remote(src, dst, send_at, recv_at, target):
        return pltpu.make_async_remote_copy(
            src_ref=src,
            dst_ref=dst,
            send_sem=send_at,
            recv_sem=recv_at,
            device_id=target,
            device_id_type=MESH,
        )

    def token_copy(d):
        return remote(
            tok_ref, zt.at[d], zt_send.at[d], zt_recv.at[d], (p, (z + d) % ex_count)
        )

    def meta_copy(d):
        target = (z + d) % ex_count
        return remote(meta_ref.at[target], zm.at[d], zm_send.at[d], zm_recv.at[d], (p, target))

    def pair_token_copy(t, src):
        return remote(src, xt.at[t], xt_send.at[t], xt_recv.at[t], (first, z))

    def pair_meta_copy(t):
        return remote(zm.at[t, 1], xm.at[t], xm_send.at[t], xm_recv.at[t], (first, z))

    def pair_partial_copy(t):
        return remote(
            recv.at[t, pl.ds(0, tok_dev)], pret.at[t], pret_send.at[t], pret_recv.at[t], (first, z)
        )

    def plane_partial_copy(t):
        return remote(
            recv.at[t, pl.ds(tok_dev, tok_dev)],
            zret.at[t - 1],
            zret_send.at[t],
            zret_recv.at[t],
            (p, (z + ex_count - t) % ex_count),
        )

    def wait_for(ref, sem):
        pltpu.make_async_copy(ref, ref, sem).wait()

    pair_token_copy(0, tok_ref).start()
    for d in range(1, ex_count):
        meta_copy(d).start()
        token_copy(d).start()
    own_meta.wait()
    pair_meta_copy(0).start()

    def exchange(t):
        meta_copy(t).wait_recv()
        pair_meta_copy(t).start()
        token_copy(t).wait_recv()
        pair_token_copy(t, zt.at[t]).start()

    def one_hot(meta, dest, value):
        slots = lax.broadcasted_iota(jnp.int32, (cap, tok_dev), 0).astype(jnp.float32)
        return jnp.where(meta[dest : dest + 1, :] == slots, value, 0.0)

    def dispatch(t, src):
        load = pltpu.make_async_copy(src, tok.at[pl.ds(0, tok_dev)], local_sem.at[0])
        load.start()
        pair_meta_copy(t).wait_recv()
        for block, meta in enumerate((zm[t, 0], xm[t])):
            for dest in range(2 * group):
                rows = pl.ds((2 * dest + block) * cap, cap)
                hot = one_hot(meta, dest, 1.0).astype(jnp.bfloat16)
                pick[rows, pl.ds(block * tok_dev, tok_dev)] = hot
        pair_token_copy(t, src).wait_recv()
        pair = pltpu.make_async_copy(xt.at[t], tok.at[pl.ds(tok_dev, tok_dev)], local_sem.at[1])
        pair.start()
        load.wait()
        pair.wait()
        slot = lax.rem(t, 2)

        @pl.loop(0, width // col_tile)
        def _(i):
            cols = pl.ds(pl.multiple_of(i * col_tile, col_tile), col_tile)
            rows = jnp.dot(pick[...], tok[:, cols], preferred_element_type=jnp.float32)
            send[slot, :, cols] = rows.astype(jnp.bfloat16)

        def give(dest, at, target):
            remote(
                send.at[slot, section(dest)],
                recv.at[t, section(at)],
                send_sem.at[slot],
                recv_sem.at[t],
                (target, z),
            ).start()

        for member in range(group):
            give(group + member, group + c, device(row2, column2, member))
        for d in range(1, group):
            member = (c + d) % group
            give(member, c, device(a, b, member))
        keep = pltpu.make_async_copy(
            send.at[slot, section(c)], recv.at[t, section(c)], local_sem.at[0]
        )
        keep.start()
        keep.wait()

    def expert(t):
        wait_for(recv.at[t, others], recv_sem.at[t])

        @pl.loop(0, ff // ff_tile)
        def _(i):
            cols = pl.ds(pl.multiple_of(i * ff_tile, ff_tile), ff_tile)
            gate = jnp.dot(recv[t], wg[:, cols], preferred_element_type=jnp.float32)
            up = jnp.dot(recv[t], wu[:, cols], preferred_element_type=jnp.float32)
            hid[:, cols] = (gate / (1.0 + jnp.exp(-gate)) * up).astype(jnp.bfloat16)

        @pl.loop(0, width // col_tile)
        def _(i):
            cols = pl.ds(pl.multiple_of(i * col_tile, col_tile), col_tile)
            rows = jnp.dot(hid[...], wd[:, cols], preferred_element_type=jnp.float32)
            recv[t, :, cols] = rows.astype(jnp.bfloat16)

        def give_back(at, dest, target):
            remote(
                recv.at[t, section(at)],
                ret.at[t, section(dest)],
                back_send.at[t],
                back_recv.at[t],
                (target, z),
            ).start()

        for member in range(group):
            target = device(1 - a, b, member) if member % 2 == 0 else device(a, 1 - b, member)
            give_back(group + member, group + c, target)
        for d in range(1, group):
            member = (c + d) % group
            give_back(member, c, device(a, b, member))
        keep = pltpu.make_async_copy(
            recv.at[t, section(c)], ret.at[t, section(c)], local_sem.at[0]
        )
        keep.start()
        keep.wait()

    def weighted(t, block, store):
        meta = xm[t] if block else zm[t, 0]
        for dest in range(2 * group):
            weight = meta[2 * group + dest : 2 * group + dest + 1, :]
            rows = pl.ds((2 * dest + block) * cap, cap)
            share[block, rows, :] = one_hot(meta, dest, weight)
        weight = share[block].T
        high = weight.astype(jnp.bfloat16)
        low = (weight - high.astype(jnp.float32)).astype(jnp.bfloat16)

        @pl.loop(0, width // col_tile)
        def _(i):
            cols = pl.ds(pl.multiple_of(i * col_tile, col_tile), col_tile)
            rows = send[0, :, cols]
            total = jnp.dot(high, rows, preferred_element_type=jnp.float32)
            total = total + jnp.dot(low, rows, preferred_element_type=jnp.float32)
            store(cols, total)

    def combined(t, store):
        wait_for(ret.at[t, others], back_recv.at[t])
        load = pltpu.make_async_copy(ret.at[t], send.at[0], local_sem.at[0])
        load.start()
        wait_for(recv.at[t, others], back_send.at[t])
        load.wait()

        def store_pair(cols, total):
            recv[t, pl.ds(0, tok_dev), cols] = total.astype(jnp.bfloat16)

        weighted(t, 1, store_pair)
        pair_partial_copy(t).start()
        pair_partial_copy(t).wait_recv()
        weighted(t, 0, store)

    own.wait()
    dispatch(0, tok_ref)
    exchange(1)
    dispatch(1, zt.at[1])
    for load in loads:
        load.wait()

    def reuse(t):
        wait_for(send.at[lax.rem(t, 2), others], send_sem.at[lax.rem(t, 2)])

    exchange(2)
    expert(1)
    reuse(2)
    dispatch(2, zt.at[2])

    def middle(t, carry):
        exchange(t)
        reuse(t)
        dispatch(t, zt.at[t])
        expert(t - 1)
        return carry

    lax.fori_loop(3, ex_count, middle, 0)

    def last(t, carry):
        expert(lax.rem(t, ex_count))
        return carry

    lax.fori_loop(ex_count - 1, ex_count + 1, last, 0)
    for slot in range(2):
        wait_for(send.at[slot, others], send_sem.at[slot])

    def home(t, carry):
        def store(cols, total):
            total = total + pret[t, :, cols].astype(jnp.float32)
            recv[t, pl.ds(tok_dev, tok_dev), cols] = total.astype(jnp.bfloat16)

        combined(t, store)
        plane_partial_copy(t).start()
        return carry

    lax.fori_loop(1, ex_count, home, 0)

    def finish(cols, total):
        total = total + pret[0, :, cols].astype(jnp.float32)
        out_ref[:, cols] = total.astype(jnp.bfloat16)

    def finish_all(cols, total):
        for d in range(1, ex_count):
            total = total + zret[d - 1, :, cols].astype(jnp.float32)
        finish(cols, total)

    for d in range(1, ex_count):
        plane_partial_copy(d).wait_recv()
    combined(0, finish_all)

    pair_token_copy(0, tok_ref).wait_send()
    pair_meta_copy(0).wait_send()
    pair_partial_copy(0).wait_send()
    for d in range(1, ex_count):
        token_copy(d).wait_send()
        meta_copy(d).wait_send()
        pair_token_copy(d, zt.at[d]).wait_send()
        pair_meta_copy(d).wait_send()
        pair_partial_copy(d).wait_send()
        plane_partial_copy(d).wait_send()


def body(tokens, expert_ids, route_weight, w_gate, w_up, w_down):
    tok_dev, width = tokens.shape
    top_count = expert_ids.shape[1]
    ff = w_gate.shape[2]
    dp_count = lax.axis_size("dp")
    ex_count = lax.axis_size("expert")
    experts = dp_count * ex_count
    group = dp_count // 4
    needed = tok_dev * top_count * 3 // (2 * experts)
    cap = -(-needed // 16) * 16
    rows = dp_count * cap

    named = expert_ids.T[None, :, :] == jnp.arange(experts, dtype=jnp.int32)[:, None, None]
    chosen = jnp.any(named, axis=1)
    weight = jnp.sum(jnp.where(named, route_weight.T[None, :, :], 0.0), axis=1)
    index = jnp.arange(tok_dev, dtype=jnp.int32)
    before = (index[:, None] < index[None, :]).astype(jnp.bfloat16)
    slot = jnp.dot(chosen.astype(jnp.bfloat16), before, preferred_element_type=jnp.float32)
    slot = jnp.where(chosen, slot, -1.0)

    p = lax.axis_index("dp")
    c, b, a = p % group, (p // group) % 2, p // (2 * group)
    even = c % 2 == 0
    sides = []
    for side in range(2):
        for other in range(2):
            row = jnp.where(even, (a + other) % 2, (a + side) % 2)
            column = jnp.where(even, (b + side) % 2, (b + other) % 2)
            sides.append((row * 2 + column) * group + jnp.arange(group))
    order = jnp.concatenate(sides)

    def by_plane(v):
        v = v.reshape(dp_count, ex_count, tok_dev)[order]
        return v.reshape(2, 2 * group, ex_count, tok_dev).transpose(2, 0, 1, 3)

    meta = jnp.concatenate([by_plane(slot), by_plane(weight)], axis=2)

    any_space = pl.BlockSpec(memory_space=pl.ANY)
    vmem = pl.BlockSpec(memory_space=pltpu.VMEM)
    dma = pltpu.SemaphoreType.DMA
    each = dma((ex_count,))
    out, _, _, _ = pl.pallas_call(
        functools.partial(kernel, dp_count, ex_count, cap),
        out_shape=(
            jax.ShapeDtypeStruct((tok_dev, width), jnp.bfloat16),
            jax.ShapeDtypeStruct((ex_count, tok_dev, width), jnp.bfloat16),
            jax.ShapeDtypeStruct((ex_count, tok_dev, width), jnp.bfloat16),
            jax.ShapeDtypeStruct((ex_count, rows, width), jnp.bfloat16),
        ),
        in_specs=[any_space, any_space, any_space, any_space, any_space],
        out_specs=(vmem, any_space, any_space, any_space),
        scratch_shapes=[
            pltpu.VMEM((width, ff), jnp.bfloat16),
            pltpu.VMEM((width, ff), jnp.bfloat16),
            pltpu.VMEM((ff, width), jnp.bfloat16),
            pltpu.VMEM((ex_count, 2, 4 * group, tok_dev), jnp.float32),
            pltpu.VMEM((ex_count, 4 * group, tok_dev), jnp.float32),
            pltpu.VMEM((rows, 2 * tok_dev), jnp.bfloat16),
            pltpu.VMEM((2, rows, tok_dev), jnp.float32),
            pltpu.VMEM((2 * tok_dev, width), jnp.bfloat16),
            pltpu.VMEM((2, rows, width), jnp.bfloat16),
            pltpu.VMEM((ex_count, rows, width), jnp.bfloat16),
            pltpu.VMEM((rows, ff), jnp.bfloat16),
            pltpu.VMEM((ex_count, tok_dev, width), jnp.bfloat16),
            pltpu.VMEM((ex_count - 1, tok_dev, width), jnp.bfloat16),
            dma((3,)),
            dma((2,)),
            each,
            each,
            each,
            each,
            each,
            each,
            each,
            each,
            dma((2,)),
            each,
            each,
            each,
            each,
            each,
            each,
            each,
        ],
        compiler_params=pltpu.CompilerParams(
            collective_id=0, has_side_effects=True, vmem_limit_bytes=60 * 1024 * 1024
        ),
        cost_estimate=pl.CostEstimate(
            flops=6 * ex_count * rows * width * ff,
            bytes_accessed=6 * width * ff + 6 * ex_count * rows * width,
            transcendentals=ex_count * rows * ff,
        ),
    )(tokens, meta, w_gate[0], w_up[0], w_down[0])
    return out


def solution(mesh):
    placed = (
        P(("dp", "expert"), None),
        P(("dp", "expert"), None),
        P(("dp", "expert"), None),
        P(("dp", "expert"), None, None),
        P(("dp", "expert"), None, None),
        P(("dp", "expert"), None, None),
    )
    return jax.shard_map(
        body, mesh=mesh, in_specs=placed, out_specs=P(("dp", "expert"), None), check_vma=False
    )
```

time: 331 us -> 363 us (1.097)
  Pallas kernels: 322 us -> 357 us
    pallas_call x1, Pallas kernels: 322 us -> 357 us  [body(): pl.pallas_call(functools.partial(kernel, dp_count, ex_count, cap), out_sh...]
where the time goes in v2:
time: 363 us
  Pallas kernels  357 us (98%)
    pallas_call x1, Pallas kernels, body(): pl.pallas_call(functools.partial(kernel, dp_count, ex_count, cap), out_sh...  357 us

profile of v2, /device:TPU:0, one launch (start us, length us, event | category | flops | bytes accessed | tf_op | source)
XLA Modules:
  0.0 362.7 jit_solution(13274693506910040617)
XLA Ops:
  0.0 0.1 fusion.1
  0.1 0.7 fusion
  0.8 0.1 convolution_select_fusion
  1.0 0.6 gather_fusion
  1.6 0.8 select_reduce_fusion
  2.3 0.6 gather_fusion.1
  2.9 0.6 pad_maximum_fusion.meta_ref
  3.5 356.8 %shard_map.64 = (bf16[128,4096]{1,0:T(8,128)(2,1)}, bf16[4,128,4096]{2,1,0:T(8,128)(2,1)}, bf16[4,128,4096]{2,1,0:T(8,128)(2,1)}, bf16[4,384,4096]{2,1,0:T(8,128)(2,1)}) custom-call(bf16[128,4096]{1,0:T(8,128)(2,1)} %tok_ref.1, f32[4,2,8,128]{3,2,1,0:T(8,128)} %pad_maximum_fusion.meta_ref, bf16[4096,768]{1,0:T(8,128)(2,1)} %bitcast.31, ...), custom_call_target="tpu_custom_call" | custom-call | flops 28991029248 | bytes 56623104 | tf_op jit(solution)/shard_map/pallas_call | solution.py:386
  360.4 2.3 copy.12
  (5 shorter events, 0.0 us)

commit v3 on v2

--- a/solution.py
+++ b/solution.py
@@ -89,7 +89,7 @@
     ]
     own = pltpu.make_async_copy(tok_ref, tok.at[pl.ds(0, tok_dev)], local_sem.at[0])
     own.start()
-    own_meta = pltpu.make_async_copy(meta_ref.at[z], zm.at[0], local_sem.at[1])
+    own_meta = pltpu.make_async_copy(meta_ref.at[z], zm.at[z], local_sem.at[1])
     own_meta.start()
     for load in loads:
         load.start()
@@ -113,20 +113,49 @@
             device_id_type=MESH,
         )
 
-    def token_copy(d):
-        return remote(
-            tok_ref, zt.at[d], zt_send.at[d], zt_recv.at[d], (p, (z + d) % ex_count)
-        )
+    low_half = 2 * z <= ex_count - 1
+    paired = jnp.where(low_half, 2 * z, 2 * (ex_count - 1 - z))
+
+    def source(t):
+        near = jnp.where(t % 2 == 1, z - (t + 1) // 2, z + t // 2)
+        return jnp.where(t <= paired, near, jnp.where(low_half, t, ex_count - 1 - t))
+
+    has_up, has_down = z + 1 < ex_count, z >= 1
+
+    def up_copy(src, s):
+        return remote(src, zt.at[s], zt_send.at[s], zt_recv.at[s], (p, (z + 1) % ex_count))
+
+    def down_copy(src, s, at):
+        target = (p, (z + ex_count - 1) % ex_count)
+        return remote(src, zt.at[s], zt_send.at[at], zt_recv.at[s], target)
+
+    def passed_on(s, act):
+        @pl.when(jnp.logical_and(s < z, has_up))
+        def _():
+            act(up_copy(zt.at[s], s))
+
+        @pl.when(jnp.logical_and(s > z, has_down))
+        def _():
+            act(down_copy(zt.at[s], s, s))
+
+    def sent_out(act):
+        @pl.when(has_up)
+        def _():
+            act(up_copy(tok_ref, z))
+
+        @pl.when(has_down)
+        def _():
+            act(down_copy(tok_ref, z, ex_count))
 
     def meta_copy(d):
         target = (z + d) % ex_count
-        return remote(meta_ref.at[target], zm.at[d], zm_send.at[d], zm_recv.at[d], (p, target))
+        return remote(meta_ref.at[target], zm.at[z], zm_send.at[d], zm_recv.at[z], (p, target))
 
     def pair_token_copy(t, src):
         return remote(src, xt.at[t], xt_send.at[t], xt_recv.at[t], (first, z))
 
     def pair_meta_copy(t):
-        return remote(zm.at[t, 1], xm.at[t], xm_send.at[t], xm_recv.at[t], (first, z))
+        return remote(zm.at[source(t), 1], xm.at[t], xm_send.at[t], xm_recv.at[t], (first, z))
 
     def pair_partial_copy(t):
         return remote(
@@ -134,29 +163,33 @@
         )
 
     def plane_partial_copy(t):
+        s = source(t)
+        away = (z + ex_count - s) % ex_count
         return remote(
             recv.at[t, pl.ds(tok_dev, tok_dev)],
-            zret.at[t - 1],
+            zret.at[away - 1],
             zret_send.at[t],
-            zret_recv.at[t],
-            (p, (z + ex_count - t) % ex_count),
+            zret_recv.at[away],
+            (p, s),
         )
 
     def wait_for(ref, sem):
         pltpu.make_async_copy(ref, ref, sem).wait()
 
+    sent_out(lambda copy: copy.start())
     pair_token_copy(0, tok_ref).start()
     for d in range(1, ex_count):
         meta_copy(d).start()
-        token_copy(d).start()
     own_meta.wait()
     pair_meta_copy(0).start()
 
     def exchange(t):
-        meta_copy(t).wait_recv()
+        s = source(t)
+        wait_for(zm.at[s], zm_recv.at[s])
         pair_meta_copy(t).start()
-        token_copy(t).wait_recv()
-        pair_token_copy(t, zt.at[t]).start()
+        wait_for(zt.at[s], zt_recv.at[s])
+        passed_on(s, lambda copy: copy.start())
+        pair_token_copy(t, zt.at[s]).start()
 
     def one_hot(meta, dest, value):
         slots = lax.broadcasted_iota(jnp.int32, (cap, tok_dev), 0).astype(jnp.float32)
@@ -166,7 +199,7 @@
         load = pltpu.make_async_copy(src, tok.at[pl.ds(0, tok_dev)], local_sem.at[0])
         load.start()
         pair_meta_copy(t).wait_recv()
-        for block, meta in enumerate((zm[t, 0], xm[t])):
+        for block, meta in enumerate((zm[source(t), 0], xm[t])):
             for dest in range(2 * group):
                 rows = pl.ds((2 * dest + block) * cap, cap)
                 hot = one_hot(meta, dest, 1.0).astype(jnp.bfloat16)
@@ -242,7 +275,7 @@
         keep.wait()
 
     def weighted(t, block, store):
-        meta = xm[t] if block else zm[t, 0]
+        meta = xm[t] if block else zm[source(t), 0]
         for dest in range(2 * group):
             weight = meta[2 * group + dest : 2 * group + dest + 1, :]
             rows = pl.ds((2 * dest + block) * cap, cap)
@@ -277,23 +310,30 @@
     own.wait()
     dispatch(0, tok_ref)
     exchange(1)
-    dispatch(1, zt.at[1])
+
+    @pl.when(paired >= 2)
+    def _():
+        exchange(2)
+
+    dispatch(1, zt.at[source(1)])
+
+    @pl.when(paired < 2)
+    def _():
+        exchange(2)
+
+    def reuse(t):
+        wait_for(send.at[lax.rem(t, 2), others], send_sem.at[lax.rem(t, 2)])
+
+    reuse(2)
+    dispatch(2, zt.at[source(2)])
     for load in loads:
         load.wait()
 
-    def reuse(t):
-        wait_for(send.at[lax.rem(t, 2), others], send_sem.at[lax.rem(t, 2)])
-
-    exchange(2)
-    expert(1)
-    reuse(2)
-    dispatch(2, zt.at[2])
-
     def middle(t, carry):
         exchange(t)
+        expert(t - 2)
         reuse(t)
-        dispatch(t, zt.at[t])
-        expert(t - 1)
+        dispatch(t, zt.at[source(t)])
         return carry
 
     lax.fori_loop(3, ex_count, middle, 0)
@@ -302,7 +342,7 @@
         expert(lax.rem(t, ex_count))
         return carry
 
-    lax.fori_loop(ex_count - 1, ex_count + 1, last, 0)
+    lax.fori_loop(ex_count - 2, ex_count + 1, last, 0)
     for slot in range(2):
         wait_for(send.at[slot, others], send_sem.at[slot])
 
@@ -327,16 +367,17 @@
         finish(cols, total)
 
     for d in range(1, ex_count):
-        plane_partial_copy(d).wait_recv()
+        wait_for(zret.at[d - 1], zret_recv.at[d])
     combined(0, finish_all)
 
     pair_token_copy(0, tok_ref).wait_send()
     pair_meta_copy(0).wait_send()
     pair_partial_copy(0).wait_send()
+    sent_out(lambda copy: copy.wait_send())
     for d in range(1, ex_count):
-        token_copy(d).wait_send()
+        passed_on(source(d), lambda copy: copy.wait_send())
         meta_copy(d).wait_send()
-        pair_token_copy(d, zt.at[d]).wait_send()
+        pair_token_copy(d, zt.at[source(d)]).wait_send()
         pair_meta_copy(d).wait_send()
         pair_partial_copy(d).wait_send()
         plane_partial_copy(d).wait_send()
@@ -409,7 +450,7 @@
             pltpu.VMEM((ex_count - 1, tok_dev, width), jnp.bfloat16),
             dma((3,)),
             dma((2,)),
-            each,
+            dma((ex_count + 1,)),
             each,
             each,
             each,

time: 363 us -> 346 us (0.953)
  the two profiles are of different devices: /device:TPU:0 before, /device:TPU:24 now
where the time goes in v3:
time: 346 us; the launch traced here: 345 us
  Pallas kernels  339 us (98%)
    pallas_call x1, Pallas kernels, body(): pl.pallas_call(functools.partial(kernel, dp_count, ex_count, cap), out_sh...  339 us

profile of v3, /device:TPU:24, one launch (start us, length us, event | category | flops | bytes accessed | tf_op | source)
XLA Modules:
  0.0 345.0 jit_solution(9363689492479817907)
XLA Ops:
  0.0 0.1 fusion.1
  0.1 0.7 fusion
  0.8 0.1 convolution_select_fusion
  1.0 0.6 gather_fusion
  1.6 0.8 select_reduce_fusion
  2.3 0.6 gather_fusion.1
  2.9 0.6 pad_maximum_fusion.meta_ref
  3.5 339.2 %shard_map.64 = (bf16[128,4096]{1,0:T(8,128)(2,1)}, bf16[4,128,4096]{2,1,0:T(8,128)(2,1)}, bf16[4,128,4096]{2,1,0:T(8,128)(2,1)}, bf16[4,384,4096]{2,1,0:T(8,128)(2,1)}) custom-call(bf16[128,4096]{1,0:T(8,128)(2,1)} %tok_ref.1, f32[4,2,8,128]{3,2,1,0:T(8,128)} %pad_maximum_fusion.meta_ref, bf16[4096,768]{1,0:T(8,128)(2,1)} %bitcast.31, ...), custom_call_target="tpu_custom_call" | custom-call | flops 28991029248 | bytes 56623104 | tf_op jit(solution)/shard_map/pallas_call | solution.py:427
  342.7 2.3 copy.12
  (5 shorter events, 0.0 us)

commit v4 on v3

--- a/solution.py
+++ b/solution.py
@@ -253,6 +253,7 @@
             rows = jnp.dot(hid[...], wd[:, cols], preferred_element_type=jnp.float32)
             recv[t, :, cols] = rows.astype(jnp.bfloat16)
 
+    def give_back_all(t):
         def give_back(at, dest, target):
             remote(
                 recv.at[t, section(at)],
@@ -287,25 +288,34 @@
         @pl.loop(0, width // col_tile)
         def _(i):
             cols = pl.ds(pl.multiple_of(i * col_tile, col_tile), col_tile)
-            rows = send[0, :, cols]
+            rows = send[lax.rem(t, 2), :, cols]
             total = jnp.dot(high, rows, preferred_element_type=jnp.float32)
             total = total + jnp.dot(low, rows, preferred_element_type=jnp.float32)
             store(cols, total)
 
-    def combined(t, store):
+    def left(t):
+        wait_for(recv.at[t, others], back_send.at[t])
+
+    def combine_pair(t):
         wait_for(ret.at[t, others], back_recv.at[t])
-        load = pltpu.make_async_copy(ret.at[t], send.at[0], local_sem.at[0])
+        load = pltpu.make_async_copy(ret.at[t], send.at[lax.rem(t, 2)], local_sem.at[0])
         load.start()
-        wait_for(recv.at[t, others], back_send.at[t])
         load.wait()
 
-        def store_pair(cols, total):
+        def store(cols, total):
             recv[t, pl.ds(0, tok_dev), cols] = total.astype(jnp.bfloat16)
 
-        weighted(t, 1, store_pair)
+        weighted(t, 1, store)
         pair_partial_copy(t).start()
+
+    def combine_own(t):
+        def store(cols, total):
+            total = total + pret[t, :, cols].astype(jnp.float32)
+            recv[t, pl.ds(tok_dev, tok_dev), cols] = total.astype(jnp.bfloat16)
+
         pair_partial_copy(t).wait_recv()
         weighted(t, 0, store)
+        plane_partial_copy(t).start()
 
     own.wait()
     dispatch(0, tok_ref)
@@ -332,43 +342,57 @@
     def middle(t, carry):
         exchange(t)
         expert(t - 2)
+
+        @pl.when(t > 3)
+        def _():
+            left(t - 3)
+
+        give_back_all(t - 2)
         reuse(t)
         dispatch(t, zt.at[source(t)])
         return carry
 
     lax.fori_loop(3, ex_count, middle, 0)
 
-    def last(t, carry):
-        expert(lax.rem(t, ex_count))
+    def last(i, carry):
+        t = lax.rem(ex_count - 2 + i, ex_count)
+        previous = ex_count - 3 + i
+        expert(t)
+        left(previous)
+        give_back_all(t)
+
+        @pl.when(i == 0)
+        def _():
+            for slot in range(2):
+                wait_for(send.at[slot, others], send_sem.at[slot])
+
+        def back(q, carry):
+            combine_pair(q)
+
+            @pl.when(q > 1)
+            def _():
+                combine_own(q - 1)
+
+            return carry
+
+        lax.fori_loop(jnp.where(i == 0, 1, previous), previous + 1, back, 0)
         return carry
 
-    lax.fori_loop(ex_count - 2, ex_count + 1, last, 0)
-    for slot in range(2):
-        wait_for(send.at[slot, others], send_sem.at[slot])
-
-    def home(t, carry):
-        def store(cols, total):
-            total = total + pret[t, :, cols].astype(jnp.float32)
-            recv[t, pl.ds(tok_dev, tok_dev), cols] = total.astype(jnp.bfloat16)
-
-        combined(t, store)
-        plane_partial_copy(t).start()
-        return carry
-
-    lax.fori_loop(1, ex_count, home, 0)
+    lax.fori_loop(0, 3, last, 0)
+    left(0)
+    combine_pair(0)
+    combine_own(ex_count - 1)
 
     def finish(cols, total):
         total = total + pret[0, :, cols].astype(jnp.float32)
-        out_ref[:, cols] = total.astype(jnp.bfloat16)
-
-    def finish_all(cols, total):
         for d in range(1, ex_count):
             total = total + zret[d - 1, :, cols].astype(jnp.float32)
-        finish(cols, total)
-
+        out_ref[:, cols] = total.astype(jnp.bfloat16)
+
+    pair_partial_copy(0).wait_recv()
     for d in range(1, ex_count):
         wait_for(zret.at[d - 1], zret_recv.at[d])
-    combined(0, finish_all)
+    weighted(0, 0, finish)
 
     pair_token_copy(0, tok_ref).wait_send()
     pair_meta_copy(0).wait_send()

time: 346 us -> 310 us (0.90)
  the two profiles are of different devices: /device:TPU:24 before, /device:TPU:25 now
where the time goes in v4:
time: 310 us; the launch traced here: 309 us
  Pallas kernels  303 us (98%)
  local copies, waits for them, and re-layouts  3.45 us (1%)
    pallas_call x1, Pallas kernels, body(): pl.pallas_call(functools.partial(kernel, dp_count, ex_count, cap), out_sh...  303 us

profile of v4, /device:TPU:25, one launch (start us, length us, event | category | flops | bytes accessed | tf_op | source)
XLA Modules:
  0.0 309.1 jit_solution(8967089413001524272)
XLA Ops:
  0.0 0.1 fusion.1
  0.1 0.7 fusion
  0.8 0.1 convolution_select_fusion
  1.0 0.6 gather_fusion
  1.6 0.8 select_reduce_fusion
  2.3 0.6 gather_fusion.1
  2.9 0.6 pad_maximum_fusion.meta_ref
  3.5 303.2 %shard_map.64 = (bf16[128,4096]{1,0:T(8,128)(2,1)}, bf16[4,128,4096]{2,1,0:T(8,128)(2,1)}, bf16[4,128,4096]{2,1,0:T(8,128)(2,1)}, bf16[4,384,4096]{2,1,0:T(8,128)(2,1)}) custom-call(bf16[128,4096]{1,0:T(8,128)(2,1)} %tok_ref.1, f32[4,2,8,128]{3,2,1,0:T(8,128)} %pad_maximum_fusion.meta_ref, bf16[4096,768]{1,0:T(8,128)(2,1)} %bitcast.31, ...), custom_call_target="tpu_custom_call" | custom-call | flops 28991029248 | bytes 56623104 | tf_op jit(solution)/shard_map/pallas_call | solution.py:451
  306.8 2.3 copy.12
  (5 shorter events, 0.0 us)

commit v5 on v4

--- a/solution.py
+++ b/solution.py
@@ -117,7 +117,8 @@
     paired = jnp.where(low_half, 2 * z, 2 * (ex_count - 1 - z))
 
     def source(t):
-        near = jnp.where(t % 2 == 1, z - (t + 1) // 2, z + t // 2)
+        inward = jnp.where(low_half, 1, -1)
+        near = z + inward * jnp.where(t % 2 == 1, (t + 1) // 2, -(t // 2))
         return jnp.where(t <= paired, near, jnp.where(low_half, t, ex_count - 1 - t))
 
     has_up, has_down = z + 1 < ex_count, z >= 1

time: 310 us -> 298 us (0.961)
  the two profiles are of different devices: /device:TPU:25 before, /device:TPU:0 now
where the time goes in v5:
time: 298 us; the launch traced here: 297 us
  Pallas kernels  291 us (98%)
  local copies, waits for them, and re-layouts  3.45 us (1%)
    pallas_call x1, Pallas kernels, body(): pl.pallas_call(functools.partial(kernel, dp_count, ex_count, cap), out_sh...  291 us

profile of v5, /device:TPU:0, one launch (start us, length us, event | category | flops | bytes accessed | tf_op | source)
XLA Modules:
  0.0 297.1 jit_solution(11450886159067569257)
XLA Ops:
  0.0 0.1 fusion.1
  0.1 0.7 fusion
  0.8 0.1 convolution_select_fusion
  1.0 0.6 gather_fusion
  1.6 0.8 select_reduce_fusion
  2.3 0.6 gather_fusion.1
  2.9 0.6 pad_maximum_fusion.meta_ref
  3.5 291.2 %shard_map.64 = (bf16[128,4096]{1,0:T(8,128)(2,1)}, bf16[4,128,4096]{2,1,0:T(8,128)(2,1)}, bf16[4,128,4096]{2,1,0:T(8,128)(2,1)}, bf16[4,384,4096]{2,1,0:T(8,128)(2,1)}) custom-call(bf16[128,4096]{1,0:T(8,128)(2,1)} %tok_ref.1, f32[4,2,8,128]{3,2,1,0:T(8,128)} %pad_maximum_fusion.meta_ref, bf16[4096,768]{1,0:T(8,128)(2,1)} %bitcast.31, ...), custom_call_target="tpu_custom_call" | custom-call | flops 28991029248 | bytes 56623104 | tf_op jit(solution)/shard_map/pallas_call | solution.py:452
  294.8 2.3 copy.12
  (5 shorter events, 0.0 us)
